TPU v7x, 32 devices: a whole 2x2x4 slice. The times are simulated.
32 devices in a mesh: expert: 4 (over z), tensor: 8 (over y, x, core).
Axes of the slice: x: 2, y: 2, z: 4, core: 2. Of those that a mesh axis runs over, the one named last changes fastest.
Arguments:
- tokens: bfloat16 [512, 5120], P('expert', 'tensor'), may hold values from -6 to 6
- routes: int32 [512, 6], P('expert'), may hold values from 0 to 15, all different within a row; in each aligned block of 128 rows (0 to 127, 128 to 255, ...) at most 64 rows name the same one
- gates: float32 [512, 6], P('expert'), may hold values from 0.05 to 0.35
- w_gate: bfloat16 [16, 1536, 5120], P('expert', 'tensor'), may hold values from -0.078125 to 0.078125
- w_up: bfloat16 [16, 1536, 5120], P('expert', 'tensor'), may hold values from -0.078125 to 0.078125
- w_down: bfloat16 [16, 1536, 5120], P('expert', None, 'tensor'), may hold values from -0.15625 to 0.15625
- shared_gate: bfloat16 [1536, 5120], P('tensor'), may hold values from -0.078125 to 0.078125
- shared_up: bfloat16 [1536, 5120], P('tensor'), may hold values from -0.078125 to 0.078125
- shared_down: bfloat16 [1536, 5120], P(None, 'tensor'), may hold values from -0.15625 to 0.15625
- vocab: bfloat16 [4096, 5120], P(('expert', 'tensor'))
- targets: int32 [16], replicated, may hold values from 0 to 4095
Outputs:
- layer_out: bfloat16 [512, 5120], P('expert', 'tensor')
- loglik: float32 [16], replicated
Inputs may be any that keep to these rules, and one draw needn't show every extreme that they name: `routes`: the tokens of one group name one expert at most 64 times; in every draw some group names some expert exactly 64 times.
All inputs are finite; a program needn't handle non-finite values.
Results may differ from a plain program's by a relative error of at most 0.0041.
Values may be sent and summed in bfloat16 or wider, within the bound.
A program may use at most 128 MiB of HBM per device.

v0:
```python
import jax
import jax.numpy as jnp
from jax import lax
from jax.sharding import PartitionSpec as P

EXPERTS = 16
SCORE_E = 4


def slot_tables(routes, gates, capacity):
    picks = (routes[:, :, None] == jnp.arange(EXPERTS, dtype=jnp.int32)[None, None, :]).astype(
        jnp.int32
    )
    per_token = jnp.sum(picks, axis=1)
    earlier = jnp.cumsum(per_token, axis=0) - per_token
    slots = jnp.sum(picks * earlier[:, None, :], axis=2)
    places = (slots[:, :, None] == jnp.arange(capacity, dtype=jnp.int32)[None, None, :]).astype(
        jnp.float32
    )
    picked = picks.astype(jnp.float32)
    select = jnp.einsum("ikr,iks->rsi", picked, places, precision=lax.Precision.HIGHEST)
    weigh = jnp.einsum("ikr,iks,ik->rsi", picked, places, gates, precision=lax.Precision.HIGHEST)
    return (select.astype(jnp.bfloat16), weigh)


def contract_last(left, right):
    return lax.dot_general(
        left, right, (((1,), (1,)), ((), ())), preferred_element_type=jnp.float32
    )


def shards(
    tokens, routes, gates, w_gate, w_up, w_down, shared_gate, shared_up, shared_down, vocab, targets
):
    tok_rows = tokens.shape[0]
    capacity = tok_rows // 2
    groups = lax.axis_size("expert")
    lanes = lax.axis_size("tensor")
    exp_dev = w_gate.shape[0]
    width = w_gate.shape[1]
    out_width = w_down.shape[2]
    select, weigh = slot_tables(routes, gates, capacity)
    outgoing = jnp.einsum("rsi,id->rsd", select, tokens, preferred_element_type=jnp.float32).astype(
        jnp.bfloat16
    )
    arrived = lax.all_to_all(outgoing, "expert", split_axis=0, concat_axis=1, tiled=True)
    slot_count = arrived.shape[1]
    flat_rows = arrived.reshape(exp_dev * slot_count, arrived.shape[2])
    pieces = (
        lax.all_gather(flat_rows, "tensor", axis=1, tiled=True),
        lax.all_gather(tokens, "tensor", axis=1, tiled=True),
    )
    span = pieces[0].shape[1]
    rows = pieces[0].reshape(exp_dev, slot_count, span)
    gate_acc = jnp.einsum("erw,efw->erf", rows, w_gate, preferred_element_type=jnp.float32)
    up_acc = jnp.einsum("erw,efw->erf", rows, w_up, preferred_element_type=jnp.float32)
    shared_gate_acc = contract_last(pieces[1], shared_gate)
    shared_up_acc = contract_last(pieces[1], shared_up)
    hidden_routed = (jax.nn.silu(gate_acc) * up_acc).astype(jnp.bfloat16)
    hidden_shared = (jax.nn.silu(shared_gate_acc) * shared_up_acc).astype(jnp.bfloat16)
    flat_hidden = hidden_routed.reshape(exp_dev * slot_count, width)
    pieces = (
        lax.all_gather(flat_hidden, "tensor", axis=1, tiled=True),
        lax.all_gather(hidden_shared, "tensor", axis=1, tiled=True),
    )
    span = pieces[0].shape[1]
    rows = pieces[0].reshape(exp_dev, slot_count, span)
    routed_out = jnp.einsum("erw,ewd->erd", rows, w_down, preferred_element_type=jnp.float32)
    shared_out = jnp.dot(pieces[1], shared_down, preferred_element_type=jnp.float32)
    returned = lax.all_to_all(
        routed_out.astype(jnp.bfloat16), "expert", split_axis=1, concat_axis=0, tiled=True
    )
    routed = jnp.einsum(
        "rsi,rsd->id", weigh, returned.astype(jnp.float32), precision=lax.Precision.HIGHEST
    )
    layer_out = (tokens.astype(jnp.float32) + shared_out + routed).astype(jnp.bfloat16)
    scored = layer_out[tok_rows - SCORE_E :].reshape(1, SCORE_E * out_width)
    collected = lax.all_gather(scored, ("expert", "tensor"), axis=0, tiled=True)
    full_rows = (
        collected.reshape(groups, lanes, SCORE_E, out_width)
        .transpose(0, 2, 1, 3)
        .reshape(groups * SCORE_E, lanes * out_width)
    )
    logits = contract_last(full_rows, vocab)
    exp_sums = jnp.sum(jnp.exp(logits), axis=1)
    offset = (lax.axis_index("expert") * lanes + lax.axis_index("tensor")) * vocab.shape[0]
    columns = offset + jnp.arange(vocab.shape[0], dtype=jnp.int32)
    target_part = jnp.sum(jnp.where(targets[:, None] == columns[None, :], logits, 0.0), axis=1)
    totals, target_logit = lax.psum((exp_sums, target_part), ("expert", "tensor"))
    loglik = target_logit - jnp.log(totals)
    return (layer_out, loglik)


def solution(mesh):
    placed = (
        P("expert", "tensor"),
        P("expert", None),
        P("expert", None),
        P("expert", "tensor", None),
        P("expert", "tensor", None),
        P("expert", None, "tensor"),
        P("tensor", None),
        P("tensor", None),
        P(None, "tensor"),
        P(("expert", "tensor"), None),
        P(),
    )
    return jax.shard_map(
        shards, mesh=mesh, in_specs=placed, out_specs=(P("expert", "tensor"), P()), check_vma=False
    )
```

profile of v0, /device:TPU:0, one launch (start us, length us, event | category | flops | bytes accessed | tf_op | source)
XLA Modules:
  0.0 311.0 jit_solution(248029319795555389)
XLA Ops:
  7.2 1.0 copy.24
  8.6 2.4 select_reduce_fusion
  11.0 1.2 fusion.1
  12.3 0.5 convolution_convert_fusion.1
  12.9 37.5 %all_to_all.33 = bf16[16,64,640]{2,1,0:T(8,128)(2,1)S(1)} all-to-all(bf16[16,64,640]{2,1,0:T(8,128)(2,1)S(1)} %convolution_convert_fusion.1), channel_id=1, replica_groups=mesh['expert'=4,'tensor'=8] {'expert'}, dimensions={0} | all-to-all | bytes 2621440 | tf_op jit(solution)/shard_map/all_to_all | solution.py:46
  50.3 1.2 copy.27
  51.6 62.4 %all-gather.7.cloned.1.call-done = bf16[1024,5120]{1,0:T(8,128)(2,1)} async-done(((bf16[1024,640]{1,0:T(8,128)(2,1)}), bf16[1024,5120]{1,0:T(8,128)(2,1)}) %all-gather.7.cloned.1.call-update) | async-done | bytes 10485776 | tf_op jit(solution)/shard_map/all_gather | solution.py:50
  114.0 9.8 %fusion.18 = f32[4,256,192]{1,2,0:T(8,128)S(1)} fusion(bf16[4,256,5120]{2,1,0:T(8,128)(2,1)} %bitcast.50, bf16[4,192,5120]{2,1,0:T(8,128)(2,1)} %param.14), kind=kOutput, calls=%fused_computation.35 | convolution fusion | flops 2013265920 | bytes 19136512 | tf_op jit(solution)/shard_map/erw,efw->erf/dot_general | solution.py:55
  123.8 9.9 %fusion.2 = bf16[4,24,8,256]{3,2,1,0:T(8,128)(2,1)S(1)} fusion(bf16[4,256,5120]{2,1,0:T(8,128)(2,1)} %bitcast.51, bf16[4,192,5120]{2,1,0:T(8,128)(2,1)} %param.15, f32[4,256,192]{1,2,0:T(8,128)S(1)} %fusion.18), kind=kOutput, calls=%fused_computation.7 | convolution fusion | flops 2014445568 | bytes 19529728 | tf_op jit(solution)/shard_map/erw,efw->erf/dot_general | solution.py:56
  133.6 0.8 copy.34
  135.2 31.7 %all-gather.9.cloned.1.call-done = bf16[1024,1536]{0,1:T(8,128)(2,1)} async-done(((bf16[1024,192]{0,1:T(8,128)(2,1)}), bf16[1024,1536]{0,1:T(8,128)(2,1)}) %all-gather.9.cloned.1.call-update) | async-done | bytes 3145744 | tf_op jit(solution)/shard_map/all_gather | solution.py:63
  166.9 4.6 %copy.29 = bf16[1024,1536]{1,0:T(8,128)(2,1)} copy(bf16[1024,1536]{0,1:T(8,128)(2,1)} %all-gather.9.cloned.1.call-done) | data formatting | bytes 6291456 | tf_op jit(solution)/shard_map/all_gather | solution.py:63
  171.6 6.8 %convolution_convert_fusion = bf16[4,256,640]{2,1,0:T(8,128)(2,1)S(1)} fusion(bf16[4,256,1536]{2,1,0:T(8,128)(2,1)} %bitcast.45, bf16[4,1536,640]{2,1,0:T(8,128)(2,1)} %param.16), kind=kOutput, calls=%fused_computation | convolution fusion | flops 2013921280 | bytes 12320768 | tf_op jit(solution)/shard_map/erw,ewd->erd/dot_general | solution.py:68
  178.4 2.1 copy.30
  180.5 4.7 %all-to-all-start.1 = ((bf16[4,256,640]{2,0,1:T(4,128)(2,1)}), bf16[4,256,640]{2,0,1:T(4,128)(2,1)S(1)}, u32[]{:S(2)}, u32[]{:S(2)}) async-start(bf16[4,256,640]{2,0,1:T(4,128)(2,1)} %copy.30), calls=%async_computation.1 | async-start | bytes 2621440 | tf_op jit(solution)/shard_map/all_to_all | solution.py:70
  185.3 2.7 convolution_bitcast_fusion
  188.1 5.4 %all-gather.5.cloned.1.call-done = bf16[128,5120]{1,0:T(8,128)(2,1)} async-done(((bf16[128,640]{1,0:T(8,128)(2,1)}), bf16[128,5120]{1,0:T(8,128)(2,1)}) %all-gather.5.cloned.1.call-update) | async-done | bytes 1310736 | tf_op jit(solution)/shard_map/all_gather | solution.py:51
  193.5 2.8 fusion.17
  196.4 0.7 fusion.5
  197.1 10.5 %all_gather.16 = bf16[128,1536]{0,1:T(8,128)(2,1)} all-gather(bf16[128,192]{0,1:T(8,128)(2,1)S(1)} %fusion.5), channel_id=1, replica_groups=mesh['expert'=4,'tensor'=8] {'tensor'}, dimensions={1}, use_global_device_ids=true | all-gather | bytes 442368 | tf_op jit(solution)/shard_map/all_gather | solution.py:64
  207.6 9.4 %all-to-all-done.1 = bf16[4,256,640]{2,0,1:T(4,128)(2,1)S(1)} async-done(((bf16[4,256,640]{2,0,1:T(4,128)(2,1)}), bf16[4,256,640]{2,0,1:T(4,128)(2,1)S(1)}, u32[]{:S(2)}, u32[]{:S(2)}) %all-to-all-start.1) | async-done | bytes 1310752 | tf_op jit(solution)/shard_map/all_to_all | solution.py:70
  217.2 1.0 copy-done.7
  218.2 1.2 convolution_bitcast_fusion.1
  219.5 0.5 fusion.4
  220.0 0.7 copy-done.8
  220.7 42.2 %all-gather = bf16[32,1,2560]{2,1,0:T(2,128)(2,1)} all-gather(bf16[1,1,2560]{2,1,0:T(2,128)(2,1)S(1)} %reshape.49), channel_id=1, replica_groups=mesh['expert'=4,'tensor'=8] {'expert','tensor'}, dimensions={0}, use_global_device_ids=true | all-gather | bytes 168960 | tf_op jit(solution)/shard_map/all_gather | solution.py:78
  262.9 1.9 reduce
  264.8 0.7 reshape.47
  265.5 0.9 copy.33
  266.5 0.6 exponential_reduce_fusion
  267.0 36.9 %all-reduce = (f32[16]{0:T(128)S(1)}, f32[16]{0:T(128)S(1)}) all-reduce(f32[16]{0:T(128)S(1)} %get-tuple-element.3, f32[16]{0:T(128)S(1)} %get-tuple-element.2), channel_id=1, replica_groups=mesh['expert'=4,'tensor'=8] {'expert','tensor'}, use_global_device_ids=true, to_apply=%region_4.5 | all-reduce | flops 32 | bytes 256 | tf_op jit(solution)/shard_map/psum | solution.py:89
  303.9 0.5 log_subtract_fusion
  (39 shorter events, 1.9 us)
Async XLA Ops:
  7.2 212.3 %copy-start = (bf16[1536,640]{1,0:T(8,128)(2,1)S(1)}, bf16[1536,640]{1,0:T(8,128)(2,1)}, u32[]{:S(2)}) copy-start(bf16[1536,640]{1,0:T(8,128)(2,1)} %param.19) | copy-start | bytes 5898244
  7.2 5.1 %copy-start.4 = (bf16[128,640]{1,0:T(8,128)(2,1)S(1)}, bf16[128,640]{1,0:T(8,128)(2,1)}, u32[]{:S(2)}) copy-start(bf16[128,640]{1,0:T(8,128)(2,1)} %param.11) | copy-start | bytes 491524
  7.2 106.8 %all-gather.7.cloned.1.call-start = ((), (), s32[]{:S(2)}) async-start(), calls=%async_computation.3 | async-start | bytes 11796480 | tf_op jit(solution)/shard_map/all_gather | solution.py:50
  11.0 1.8 copy-start.9
  51.5 115.4 %all-gather.9.cloned.1.call-start = ((), (), s32[]{:S(2)}) async-start(), calls=%async_computation.4 | async-start | bytes 3538944 | tf_op jit(solution)/shard_map/all_gather | solution.py:63
  134.5 59.0 %all-gather.5.cloned.1.call-start = ((), (), s32[]{:S(2)}) async-start(), calls=%async_computation.2 | async-start | bytes 1474560 | tf_op jit(solution)/shard_map/all_gather | solution.py:51
  180.5 4.7 %copy-start.11 = (f32[128,6]{0,1:T(8,128)S(1)}, f32[128,6]{0,1:T(8,128)}, u32[]{:S(2)}) copy-start(f32[128,6]{0,1:T(8,128)} %param.13) | copy-start | bytes 9220
  180.5 4.8 %copy-start.10 = (s32[128,6]{1,0:T(8,128)S(1)}, s32[128,6]{1,0:T(8,128)}, u32[]{:S(2)}) copy-start(s32[128,6]{1,0:T(8,128)} %copy-done.9) | copy-start | bytes 9220
  180.5 36.5 %all-to-all-start.1 = ((bf16[4,256,640]{2,0,1:T(4,128)(2,1)}), bf16[4,256,640]{2,0,1:T(4,128)(2,1)S(1)}, u32[]{:S(2)}, u32[]{:S(2)}) async-start(bf16[4,256,640]{2,0,1:T(4,128)(2,1)} %copy.30), calls=%async_computation.1 | async-start | bytes 2621440 | tf_op jit(solution)/shard_map/all_to_all | solution.py:70
  193.5 2.8 copy-start.1
  193.5 2.9 copy-start.2
  217.0 1.2 copy-start.7
  217.2 2.3 copy-start.3
  217.2 2.3 copy-start.5
  219.5 47.0 %copy-start.6 = (bf16[128,5120]{1,0:T(8,128)(2,1)S(1)}, bf16[128,5120]{1,0:T(8,128)(2,1)}, u32[]{:S(2)}) copy-start(bf16[128,5120]{1,0:T(8,128)(2,1)} %param.20) | copy-start | bytes 3932164
  219.5 47.0 %copy-start.12 = (s32[16]{0:T(128)S(1)}, s32[16]{0:T(128)}, u32[]{:S(2)}) copy-start(s32[16]{0:T(128)} %param.21) | copy-start | bytes 196
  220.0 0.7 copy-start.8
Sparse Core Ops, SparseCore 0:
  51.7 62.2 all-gather.6
  134.6 32.3 all-gather.8
  168.8 24.5 all-gather.4
where the time goes:
time: 312 us; the launch traced here: 311 us
  blocking collectives  127 us (41%)
  waiting for transfers between devices  109 us (35%)
  matrix products  36.8 us (12%)
  between operations  14 us (4%)
  local copies, waits for them, and re-layouts  13.5 us (4%)
  other arithmetic  5.23 us (2%)
  starting transfers between devices  5.01 us (2%)
    all_gather x1, waiting for transfers between devices, shards(): lax.all_gather(flat_rows, 'tensor', axis=1, tiled=True)  62.4 us
    all_gather x1, blocking collectives, shards(): collected = lax.all_gather(scored, ('expert', 'tensor'), axis=0, tiled=True)  42.2 us
    all_to_all x1, blocking collectives, shards(): lax.all_to_all(outgoing, 'expert', split_axis=0, concat_axis=1, tiled=True)  37.5 us
    psum x1, blocking collectives, shards(): lax.psum((exp_sums, target_part), ('expert', 'tensor'))  36.9 us
    all_gather x1, waiting for transfers between devices, shards(): lax.all_gather(flat_hidden, 'tensor', axis=1, tiled=True)  31.7 us
    all_gather x1, blocking collectives, shards(): lax.all_gather(hidden_shared, 'tensor', axis=1, tiled=True)  10.5 us
    dot_general x1, matrix products, shards(): jnp.einsum('erw,efw->erf', rows, w_up, preferred_element_type=jnp.float32)  9.88 us
    dot_general x1, matrix products, shards(): jnp.einsum('erw,efw->erf', rows, w_gate, preferred_element_type=jnp.float32)  9.81 us
  transfers between devices with their start and end apart: 4, of which 4 were waited for; matrix products, arithmetic and copies ran while one was open for 6% of the time, Pallas kernels for 0%

commit v1 on v0

--- a/solution.py
+++ b/solution.py
@@ -1,6 +1,8 @@
 import jax
 import jax.numpy as jnp
 from jax import lax
+from jax.experimental import pallas as pl
+from jax.experimental.pallas import tpu as pltpu
 from jax.sharding import PartitionSpec as P
 
 EXPERTS = 16
@@ -91,6 +93,422 @@
     return (layer_out, loglik)
 
 
+MESH_ID = pl.DeviceIdType.MESH
+CHUNK_COPIES = 9
+NT = (((1,), (1,)), ((), ()))
+
+
+def flip(index, low):
+    return index + low - 2 * low * lax.rem(lax.div(index, low), 2)
+
+
+def z_peer(z, j):
+    for low in (1, 2):
+        if j & low:
+            z = flip(z, low)
+    return z
+
+
+def t_peer(t, j):
+    for low in (1, 2, 4):
+        if j & low:
+            t = flip(t, low)
+    return t
+
+
+def silu_mul(gate, up):
+    return gate / (1.0 + jnp.exp(-gate)) * up
+
+
+def layer_kernel(
+    tokens, routes_t, gates_t, w_gate, w_up, w_down, shared_gate, shared_up, shared_down, vocab, targets,
+    out, loglik,
+    wg, wu, wd, sg, su, sd, vo, tok, acc_g, acc_u, sh_g, sh_u, hid, out_acc, sh_out, tab, part_out, part_in,
+    sc, full, st_t, st_z,
+    load_sem, ch_send, ch_recv, z_send, z_recv, t_send, t_recv,
+):
+    z, t = lax.axis_index("expert"), lax.axis_index("tensor")
+    rows, cols = tokens.shape
+    cap = rows // 2
+    ff = sg.shape[0]
+
+    loads = []
+    pairs = (
+        (tokens, tok.at[t, pl.ds(z * rows, rows)]), (shared_gate, sg), (shared_up, su), (w_gate, wg), (w_up, wu),
+        (w_down, wd), (shared_down, sd), (vocab, vo),
+    )
+    for i, (a, b) in enumerate(pairs):
+        loads.append(pltpu.make_async_copy(a, b, load_sem.at[i]))
+        loads[-1].start()
+
+    barrier = pltpu.get_barrier_semaphore()
+    for j in range(1, 4):
+        pl.semaphore_signal(barrier, inc=1, device_id=(z_peer(z, j), t), device_id_type=MESH_ID)
+    for j in range(1, 8):
+        pl.semaphore_signal(barrier, inc=1, device_id=(z, t_peer(t, j)), device_id_type=MESH_ID)
+
+    experts = tab.shape[2]
+    expert_row = lax.broadcasted_iota(jnp.int32, (experts, rows), 0)
+    member = jnp.zeros((experts, rows), jnp.float32)
+    weight = jnp.zeros((experts, rows), jnp.float32)
+    for k in range(routes_t.shape[0]):
+        hit = routes_t[k : k + 1, :] == expert_row
+        member = jnp.where(hit, 1.0, member)
+        weight = jnp.where(hit, gates_t[k : k + 1, :], weight)
+    before = lax.broadcasted_iota(jnp.int32, (rows, rows), 0) < lax.broadcasted_iota(jnp.int32, (rows, rows), 1)
+    earlier = jnp.dot(
+        member.astype(jnp.bfloat16),
+        jnp.where(before, 1.0, 0.0).astype(jnp.bfloat16),
+        preferred_element_type=jnp.float32,
+    )
+    tab[0, 0] = jnp.where(member > 0.5, earlier, -1.0)
+    tab[0, 1] = weight
+
+    pl.semaphore_wait(barrier, 10)
+
+    sends = []
+
+    def send(src, dst, ssem, rsem, dev):
+        copy = pltpu.make_async_remote_copy(
+            src_ref=src, dst_ref=dst, send_sem=ssem, recv_sem=rsem, device_id=dev, device_id_type=MESH_ID
+        )
+        copy.start()
+        sends.append(copy)
+
+    def landed(dst, rsem):
+        pltpu.make_async_remote_copy(
+            src_ref=dst, dst_ref=dst, send_sem=ch_send.at[0], recv_sem=rsem, device_id=(z, t_peer(t, 1)),
+            device_id_type=MESH_ID,
+        ).wait_recv()
+
+    t_c, t_x, t_y, t_d = t_peer(t, 1), t_peer(t, 2), t_peer(t, 4), t_peer(t, 6)
+
+    class Chunk:
+        def __init__(self, number, buf, start, count):
+            self.base, self.buf, self.first, self.count = number * CHUNK_COPIES, buf, start, count
+
+        def part(self, owner, which=None):
+            if which is None:
+                return self.buf.at[owner, pl.ds(self.first, self.count)]
+            half = self.count // 2
+            return self.buf.at[owner, pl.ds(self.first + which * half, half)]
+
+        def go(self, ref, n, peer):
+            send(ref, ref, ch_send.at[self.base + n], ch_recv.at[self.base + n], (z, peer))
+
+        def got(self, ref, n):
+            landed(ref, ch_recv.at[self.base + n])
+
+        def start(self):
+            for n, peer in ((0, t_x), (1, t_y), (2, t_c)):
+                self.go(self.part(t), n, peer)
+
+        def relay(self):
+            self.got(self.part(t_x), 0)
+            self.go(self.part(t_x, 0), 3, t_y)
+            self.go(self.part(t_x), 4, t_c)
+            self.got(self.part(t_y), 1)
+            self.go(self.part(t_y, 1), 5, t_x)
+            self.go(self.part(t_y), 6, t_c)
+
+        def relay_far(self):
+            self.got(self.part(t_d, 0), 3)
+            self.go(self.part(t_d, 0), 7, t_c)
+            self.got(self.part(t_d, 1), 5)
+            self.go(self.part(t_d, 1), 8, t_c)
+
+        def wait_own(self):
+            self.got(self.part(t_c), 2)
+
+        def wait_x(self):
+            self.got(self.part(t_peer(t, 3)), 4)
+
+        def wait_y(self):
+            self.got(self.part(t_peer(t, 5)), 6)
+
+        def wait_far(self):
+            self.got(self.part(t_peer(t, 7), 0), 7)
+            self.got(self.part(t_peer(t, 7), 1), 8)
+
+        def finish(self):
+            self.wait_own()
+            self.wait_x()
+            self.wait_y()
+            self.wait_far()
+
+    groups = [z, z_peer(z, 1), z_peer(z, 2), z_peer(z, 3)]
+    chunks = [Chunk(k, tok, groups[k] * rows, rows) for k in range(4)]
+    far_rows, own_rows = 8 * cap // 2, 8 * cap // 2 + cap
+    hid_far = Chunk(4, hid, 0, far_rows)
+    hid_own = Chunk(5, hid, far_rows, own_rows)
+    loads[0].wait()
+    for j in (1, 2, 3):
+        mine = tok.at[t, pl.ds(z * rows, rows)]
+        send(mine, mine, z_send.at[j], z_recv.at[j], (groups[j], t))
+    for j in (1, 2, 3):
+        send(tab.at[0], tab.at[j], z_send.at[4 + j], z_recv.at[4 + j], (groups[j], t))
+    chunks[0].start()
+
+    def z_landed(j):
+        landed(chunks[j].part(t), z_recv.at[j])
+        chunks[j].start()
+
+    z_landed(1)
+    chunks[0].relay()
+    z_landed(2)
+    chunks[1].relay()
+    chunks[0].relay_far()
+    z_landed(3)
+    for load in loads[1:5]:
+        load.wait()
+    chunks[1].relay_far()
+    chunks[0].finish()
+    chunks[1].finish()
+
+    def clear():
+        acc_g[...] = jnp.zeros_like(acc_g)
+        acc_u[...] = jnp.zeros_like(acc_u)
+
+    def up_seg(pair, chip, shared):
+        def step(i, carry):
+            owner = 2 * chip + i
+            span = pl.ds(pl.multiple_of(owner * cols, 128), cols)
+            x = tok[owner, pl.ds(pl.multiple_of(pair * 2 * rows, 128), 2 * rows), :]
+            acc_g[...] += lax.dot_general(x, wg[:, span], NT, preferred_element_type=jnp.float32)
+            acc_u[...] += lax.dot_general(x, wu[:, span], NT, preferred_element_type=jnp.float32)
+            if shared:
+                own = tok[owner, pl.ds(pl.multiple_of(z * rows, 128), rows), :]
+                sh_g[...] += lax.dot_general(own, sg[:, span], NT, preferred_element_type=jnp.float32)
+                sh_u[...] += lax.dot_general(own, su[:, span], NT, preferred_element_type=jnp.float32)
+            return carry
+
+        lax.fori_loop(0, 2, step, 0)
+
+    slot_no = lax.broadcasted_iota(jnp.int32, (cap, rows), 0).astype(jnp.float32)
+
+    def table_of(j):
+        first = pl.ds(4 * z, 4)
+        return tab[j, 0, first, :], tab[j, 1, first, :]
+
+    def squeeze(first_row, js):
+        for j in js:
+            place = lax.rem(groups[j], 2)
+            span = pl.ds(pl.multiple_of(place * rows, 128), rows)
+            h = silu_mul(acc_g[span, :], acc_u[span, :]).astype(jnp.bfloat16)
+            slots, _ = table_of(j)
+            for q in range(2):
+                both = h[:, 2 * q * ff : 2 * (q + 1) * ff]
+                picked = []
+                for e in (2 * q, 2 * q + 1):
+                    sel = jnp.where(slot_no == slots[e : e + 1, :], 1.0, 0.0).astype(jnp.bfloat16)
+                    picked.append(jnp.dot(sel, both, preferred_element_type=jnp.float32))
+                lane = lax.broadcasted_iota(jnp.int32, picked[0].shape, 1)
+                at = pl.ds(pl.multiple_of(first_row + q * 2 * cap + place * cap, 16), cap)
+                hid[t, at, :] = jnp.where(lane < ff, picked[0], picked[1]).astype(jnp.bfloat16)
+
+    chip, chip_x, chip_y, chip_d = [lax.div(v, 2) for v in (t, t_x, t_y, t_d)]
+    own_pair, far_pair = lax.div(z, 2), 1 - lax.div(z, 2)
+    clear()
+    sh_g[...] = jnp.zeros_like(sh_g)
+    sh_u[...] = jnp.zeros_like(sh_u)
+    up_seg(own_pair, chip, True)
+    chunks[2].relay()
+    up_seg(own_pair, chip_x, True)
+    up_seg(own_pair, chip_y, True)
+    chunks[3].relay()
+    chunks[2].relay_far()
+    up_seg(own_pair, chip_d, True)
+    for j in (1, 2, 3):
+        landed(tab.at[j], z_recv.at[4 + j])
+    squeeze(far_rows, (0, 1))
+    hs = silu_mul(sh_g[...], sh_u[...])
+    hid[t, pl.ds(2 * far_rows, cap), :] = jnp.concatenate([hs[:cap], hs[cap:]], axis=1).astype(jnp.bfloat16)
+    clear()
+    chunks[3].relay_far()
+    for c in (2, 3):
+        chunks[c].wait_own()
+    up_seg(far_pair, chip, False)
+    for c in (2, 3):
+        chunks[c].wait_x()
+    up_seg(far_pair, chip_x, False)
+    for c in (2, 3):
+        chunks[c].wait_y()
+    up_seg(far_pair, chip_y, False)
+    for c in (2, 3):
+        chunks[c].wait_far()
+    up_seg(far_pair, chip_d, False)
+    squeeze(0, (2, 3))
+    hid_far.start()
+    hid_own.start()
+    for load in loads[5:]:
+        load.wait()
+
+    def down_seg(first_row, chip_no, shared):
+        def step(i, carry):
+            owner = 2 * chip_no + i
+            span = pl.ds(pl.multiple_of(owner * ff, 16), ff)
+            for q in range(2):
+                h = hid[owner, pl.ds(first_row + q * 2 * cap, 2 * cap), :]
+                for k in range(2):
+                    out_acc[2 * q + k] += jnp.dot(
+                        h[:, k * ff : (k + 1) * ff], wd[2 * q + k, span, :], preferred_element_type=jnp.float32
+                    )
+            if shared:
+                h = hid[owner, pl.ds(2 * far_rows, cap), :]
+                for k in range(2):
+                    sh_out[k * cap : (k + 1) * cap, :] += jnp.dot(
+                        h[:, k * ff : (k + 1) * ff], sd[span, :], preferred_element_type=jnp.float32
+                    )
+            return carry
+
+        lax.fori_loop(0, 2, step, 0)
+
+    def combine(j):
+        place = lax.rem(groups[j], 2)
+        span = pl.ds(pl.multiple_of(place * cap, 16), cap)
+        slots, weights = table_of(j)
+        ys = jnp.concatenate([out_acc[e, span, :].astype(jnp.bfloat16) for e in range(4)], axis=0)
+        mix = jnp.concatenate(
+            [jnp.where(slot_no == slots[e : e + 1, :], weights[e : e + 1, :], 0.0) for e in range(4)], axis=0
+        ).T
+        high = mix.astype(jnp.bfloat16)
+        low = (mix - high.astype(jnp.float32)).astype(jnp.bfloat16)
+        return jnp.dot(high, ys, preferred_element_type=jnp.float32) + jnp.dot(
+            low, ys, preferred_element_type=jnp.float32
+        )
+
+    def give(j):
+        part_out[j] = combine(j).astype(jnp.bfloat16)
+        send(part_out.at[j], part_in.at[j], z_send.at[8 + j], z_recv.at[8 + j], (groups[j], t))
+
+    out_acc[...] = jnp.zeros_like(out_acc)
+    sh_out[...] = jnp.zeros_like(sh_out)
+    hid_far.wait_own()
+    down_seg(0, chip, False)
+    hid_far.relay()
+    hid_far.wait_x()
+    down_seg(0, chip_x, False)
+    hid_far.relay_far()
+    hid_far.wait_y()
+    down_seg(0, chip_y, False)
+    hid_far.wait_far()
+    down_seg(0, chip_d, False)
+    hid_own.relay()
+    give(2)
+    give(3)
+    out_acc[...] = jnp.zeros_like(out_acc)
+    hid_own.wait_own()
+    down_seg(far_rows, chip, True)
+    hid_own.relay_far()
+    hid_own.wait_x()
+    down_seg(far_rows, chip_x, True)
+    hid_own.wait_y()
+    down_seg(far_rows, chip_y, True)
+    hid_own.wait_far()
+    down_seg(far_rows, chip_d, True)
+    give(1)
+    total = tok[t, pl.ds(pl.multiple_of(z * rows, 128), rows), :].astype(jnp.float32) + sh_out[...] + combine(0)
+    for j in (1, 2, 3):
+        landed(part_in.at[j], z_recv.at[8 + j])
+        total += part_in[j].astype(jnp.float32)
+    layer = total.astype(jnp.bfloat16)
+    out[...] = layer
+
+    sc[z] = layer[rows - 16 :, :]
+    for j in (1, 2, 3):
+        send(sc.at[z], sc.at[z], z_send.at[12 + j], z_recv.at[12 + j], (groups[j], t))
+    for j in (1, 2, 3):
+        landed(sc.at[groups[j]], z_recv.at[12 + j])
+    full[t] = jnp.concatenate(
+        [sc[g].astype(jnp.float32)[16 - SCORE_E :, :] for g in range(4)], axis=0
+    ).astype(jnp.bfloat16)
+    for j in range(1, 8):
+        send(full.at[t], full.at[t], t_send.at[j], t_recv.at[j], (z, t_peer(t, j)))
+    logits = jnp.zeros((vo.shape[0], full.shape[1]), jnp.float32)
+    for j in range(8):
+        owner = t_peer(t, j)
+        if j:
+            landed(full.at[owner], t_recv.at[j])
+        span = pl.ds(pl.multiple_of(owner * cols, 128), cols)
+        logits += lax.dot_general(vo[:, span], full[owner], NT, preferred_element_type=jnp.float32)
+    offset = (z * 8 + t) * vo.shape[0]
+    entry = offset + lax.broadcasted_iota(jnp.int32, logits.shape, 0)
+    st_t[0] = jnp.zeros_like(st_t[0])
+    st_t[0, 0:1, 0:16] = jnp.sum(jnp.exp(logits), axis=0, keepdims=True)
+    st_t[0, 1:2, 0:16] = jnp.sum(jnp.where(entry == targets[...], logits, 0.0), axis=0, keepdims=True)
+    for j in range(1, 8):
+        send(st_t.at[0], st_t.at[j], t_send.at[8 + j], t_recv.at[8 + j], (z, t_peer(t, j)))
+    summed = st_t[0]
+    for j in range(1, 8):
+        landed(st_t.at[j], t_recv.at[8 + j])
+        summed += st_t[j]
+    st_z[z] = summed
+    for j in (1, 2, 3):
+        send(st_z.at[z], st_z.at[z], z_send.at[16 + j], z_recv.at[16 + j], (groups[j], t))
+    for j in (1, 2, 3):
+        landed(st_z.at[groups[j]], z_recv.at[16 + j])
+    both = ((st_z[0] + st_z[1]) + st_z[2]) + st_z[3]
+    loglik[...] = both[1:2, 0:16] - jnp.log(both[0:1, 0:16])
+    for copy in sends:
+        copy.wait_send()
+
+
+def fused_shards(
+    tokens, routes, gates, w_gate, w_up, w_down, shared_gate, shared_up, shared_down, vocab, targets
+):
+    rows, cols = tokens.shape
+    own, ff, depth = w_gate.shape
+    cap = rows // 2
+    far_rows = 4 * cap
+    bf, f32 = jnp.bfloat16, jnp.float32
+    hbm, vmem = pl.BlockSpec(memory_space=pl.ANY), pl.BlockSpec(memory_space=pltpu.VMEM)
+    dma = pltpu.SemaphoreType.DMA
+    out, loglik = pl.pallas_call(
+        layer_kernel,
+        out_shape=(jax.ShapeDtypeStruct((rows, cols), bf), jax.ShapeDtypeStruct((1, targets.shape[0]), f32)),
+        in_specs=[hbm, vmem, vmem, hbm, hbm, hbm, hbm, hbm, hbm, hbm, vmem],
+        out_specs=(vmem, vmem),
+        scratch_shapes=[
+            pltpu.VMEM((own * ff, depth), bf),
+            pltpu.VMEM((own * ff, depth), bf),
+            pltpu.VMEM(w_down.shape, bf),
+            pltpu.VMEM(shared_gate.shape, bf),
+            pltpu.VMEM(shared_up.shape, bf),
+            pltpu.VMEM(shared_down.shape, bf),
+            pltpu.VMEM(vocab.shape, bf),
+            pltpu.VMEM((8, 4 * rows, cols), bf),
+            pltpu.VMEM((2 * rows, own * ff), f32),
+            pltpu.VMEM((2 * rows, own * ff), f32),
+            pltpu.VMEM((rows, ff), f32),
+            pltpu.VMEM((rows, ff), f32),
+            pltpu.VMEM((8, 2 * far_rows + cap, 2 * ff), bf),
+            pltpu.VMEM((own, 2 * cap, cols), f32),
+            pltpu.VMEM((rows, cols), f32),
+            pltpu.VMEM((4, 2, EXPERTS, rows), f32),
+            pltpu.VMEM((4, rows, cols), bf),
+            pltpu.VMEM((4, rows, cols), bf),
+            pltpu.VMEM((4, 16, cols), bf),
+            pltpu.VMEM((8, 4 * SCORE_E, cols), bf),
+            pltpu.VMEM((8, 8, 128), f32),
+            pltpu.VMEM((4, 8, 128), f32),
+            dma((8,)),
+            dma((6 * CHUNK_COPIES,)),
+            dma((6 * CHUNK_COPIES,)),
+            dma((20,)),
+            dma((20,)),
+            dma((16,)),
+            dma((16,)),
+        ],
+        compiler_params=pltpu.CompilerParams(
+            collective_id=0, has_side_effects=True, vmem_limit_bytes=60 * 2**20
+        ),
+    )(
+        tokens, routes.T, gates.T, w_gate.reshape(own * ff, depth), w_up.reshape(own * ff, depth), w_down,
+        shared_gate, shared_up, shared_down, vocab, targets.reshape(1, -1),
+    )
+    return out, loglik.reshape(-1)
+
+
 def solution(mesh):
     placed = (
         P("expert", "tensor"),
@@ -105,6 +523,7 @@
         P(("expert", "tensor"), None),
         P(),
     )
+    fits = mesh.shape["expert"] == 4 and mesh.shape["tensor"] == 8
     return jax.shard_map(
-        shards, mesh=mesh, in_specs=placed, out_specs=(P("expert", "tensor"), P()), check_vma=False
-    )
+        fused_shards if fits else shards, mesh=mesh, in_specs=placed, out_specs=(P("expert", "tensor"), P()), check_vma=False
+    )

time: 312 us -> 94.6 us (0.30)
  blocking collectives: 127 us -> 0 us
  waiting for transfers between devices: 109 us -> 0 us
  Pallas kernels: 0 us -> 91 us
  matrix products: 36.8 us -> 0 us
  between operations: 14 us -> 0.64 us
  local copies, waits for them, and re-layouts: 13.5 us -> 2.73 us
  other arithmetic: 5.23 us -> 0 us
  starting transfers between devices: 5.01 us -> 0 us
    all_gather x3 -> x0, waiting for transfers between devices: 99.5 us -> none  [the longest x1 62.4 us: shards(): lax.all_gather(flat_rows, 'tensor', axis=1, tiled=True)]
    pallas_call x0 -> x1, Pallas kernels: none -> 91 us  [fused_shards(): pl.pallas_call(layer_kernel, out_shape=(jax.ShapeDtypeStruct((rows, cols)...]
    all_gather x2 -> x0, blocking collectives: 52.7 us -> none  [the longest x1 42.2 us: shards(): collected = lax.all_gather(scored, ('expert', 'tensor'), axis=0, tiled=True)]
    all_to_all x1 -> x0, blocking collectives: 37.5 us -> none  [shards(): lax.all_to_all(outgoing, 'expert', split_axis=0, concat_axis=1, tiled=True)]
    psum x1 -> x0, blocking collectives: 36.9 us -> none  [shards(): lax.psum((exp_sums, target_part), ('expert', 'tensor'))]
    dot_general x11 -> x0, matrix products: 36.8 us -> none  [the longest x1 9.88 us: shards(): jnp.einsum('erw,efw->erf', rows, w_up, preferred_element_type=jnp.float32)]
    all_to_all x1 -> x0, waiting for transfers between devices: 9.36 us -> none  [shards(): lax.all_to_all(routed_out.astype(jnp.bfloat16), 'expert', split_axis=1, c...]
    all_to_all x1 -> x0, starting transfers between devices: 4.7 us -> none  [shards(): lax.all_to_all(routed_out.astype(jnp.bfloat16), 'expert', split_axis=1, c...]
  transfers between devices with their start and end apart: 4 -> 0, of which waited for: 4 -> 0; matrix products, arithmetic and copies ran while one was open for 6% -> 0% of each run, Pallas kernels for 0% -> 0%
where the time goes in v1:
time: 94.6 us; the launch traced here: 94.4 us
  Pallas kernels  91 us (96%)
  local copies, waits for them, and re-layouts  2.73 us (3%)
    pallas_call x1, Pallas kernels, fused_shards(): pl.pallas_call(layer_kernel, out_shape=(jax.ShapeDtypeStruct((rows, cols)...  91 us
    unnamed x2, local copies, waits for them, and re-layouts  2.73 us

profile of v1, /device:TPU:0, one launch (start us, length us, event | category | flops | bytes accessed | tf_op | source)
XLA Modules:
  0.0 94.4 jit_solution(13359543898097851815)
XLA Ops:
  0.6 91.0 %shard_map.122 = (bf16[128,640]{1,0:T(8,128)(2,1)}, f32[1,16]{1,0:T(1,128)}) custom-call(bf16[128,640]{1,0:T(8,128)(2,1)} %tokens.1, s32[6,128]{1,0:T(8,128)} %bitcast.8, f32[6,128]{1,0:T(8,128)} %bitcast.9, bf16[768,5120]{1,0:T(8,128)(2,1)} %bitcast.6, bf16[768,5120]{1,0:T(8,128)(2,1)} %bitcast.7, bf16[4,1536,640]{2,1,0:T(8,128)(2,1)} %w_down.1, ...), custom_call_target="tpu_custom_call" | custom-call | tf_op jit(solution)/shard_map/pallas_call | solution.py:466
  91.7 1.6 %copy.15 = bf16[128,640]{1,0:T(8,128)(2,1)} copy(bf16[128,640]{1,0:T(8,128)(2,1)} %get-tuple-element.8) | data formatting | bytes 327680
  93.3 1.1 %copy.16 = f32[16]{0:T(128)} copy(f32[16]{0:T(128)} %bitcast.11) | data formatting | bytes 128

commit v2 on v1

--- a/solution.py
+++ b/solution.py
@@ -255,13 +255,11 @@
 
     z_landed(1)
     chunks[0].relay()
-    z_landed(2)
     chunks[1].relay()
     chunks[0].relay_far()
-    z_landed(3)
+    chunks[1].relay_far()
     for load in loads[1:5]:
         load.wait()
-    chunks[1].relay_far()
     chunks[0].finish()
     chunks[1].finish()
 
@@ -312,8 +310,10 @@
     sh_g[...] = jnp.zeros_like(sh_g)
     sh_u[...] = jnp.zeros_like(sh_u)
     up_seg(own_pair, chip, True)
+    z_landed(2)
+    up_seg(own_pair, chip_x, True)
+    z_landed(3)
     chunks[2].relay()
-    up_seg(own_pair, chip_x, True)
     up_seg(own_pair, chip_y, True)
     chunks[3].relay()
     chunks[2].relay_far()
@@ -377,9 +377,16 @@
             low, ys, preferred_element_type=jnp.float32
         )
 
-    def give(j):
-        part_out[j] = combine(j).astype(jnp.bfloat16)
-        send(part_out.at[j], part_in.at[j], z_send.at[8 + j], z_recv.at[8 + j], (groups[j], t))
+    ends, rest = pl.ds(rows - 16, 16), pl.ds(0, rows - 16)
+
+    def give(js):
+        for j in js:
+            part_out[j] = combine(j).astype(jnp.bfloat16)
+        for at, first in ((ends, 8), (rest, 20)):
+            for j in js:
+                send(
+                    part_out.at[j, at], part_in.at[j, at], z_send.at[first + j], z_recv.at[first + j], (groups[j], t)
+                )
 
     out_acc[...] = jnp.zeros_like(out_acc)
     sh_out[...] = jnp.zeros_like(sh_out)
@@ -394,8 +401,7 @@
     hid_far.wait_far()
     down_seg(0, chip_d, False)
     hid_own.relay()
-    give(2)
-    give(3)
+    give((2, 3))
     out_acc[...] = jnp.zeros_like(out_acc)
     hid_own.wait_own()
     down_seg(far_rows, chip, True)
@@ -406,15 +412,17 @@
     down_seg(far_rows, chip_y, True)
     hid_own.wait_far()
     down_seg(far_rows, chip_d, True)
-    give(1)
+    give((1,))
     total = tok[t, pl.ds(pl.multiple_of(z * rows, 128), rows), :].astype(jnp.float32) + sh_out[...] + combine(0)
-    for j in (1, 2, 3):
-        landed(part_in.at[j], z_recv.at[8 + j])
-        total += part_in[j].astype(jnp.float32)
-    layer = total.astype(jnp.bfloat16)
-    out[...] = layer
-
-    sc[z] = layer[rows - 16 :, :]
+    last = total[rows - 16 :, :]
+    sh_out[...] = total
+    for j in (1, 2, 3):
+        landed(part_in.at[j, ends], z_recv.at[8 + j])
+        last += part_in[j, rows - 16 :, :].astype(jnp.float32)
+    layer_end = last.astype(jnp.bfloat16)
+    out[rows - 16 :, :] = layer_end
+
+    sc[z] = layer_end
     for j in (1, 2, 3):
         send(sc.at[z], sc.at[z], z_send.at[12 + j], z_recv.at[12 + j], (groups[j], t))
     for j in (1, 2, 3):
@@ -445,6 +453,11 @@
     st_z[z] = summed
     for j in (1, 2, 3):
         send(st_z.at[z], st_z.at[z], z_send.at[16 + j], z_recv.at[16 + j], (groups[j], t))
+    body = sh_out[0 : rows - 16, :]
+    for j in (1, 2, 3):
+        landed(part_in.at[j, rest], z_recv.at[20 + j])
+        body += part_in[j, 0 : rows - 16, :].astype(jnp.float32)
+    out[0 : rows - 16, :] = body.astype(jnp.bfloat16)
     for j in (1, 2, 3):
         landed(st_z.at[groups[j]], z_recv.at[16 + j])
     both = ((st_z[0] + st_z[1]) + st_z[2]) + st_z[3]
@@ -494,8 +507,8 @@
             dma((8,)),
             dma((6 * CHUNK_COPIES,)),
             dma((6 * CHUNK_COPIES,)),
-            dma((20,)),
-            dma((20,)),
+            dma((24,)),
+            dma((24,)),
             dma((16,)),
             dma((16,)),
         ],

time: 94.6 us -> 95.6 us (1.011)
  Pallas kernels: 91 us -> 92 us
    pallas_call x1, Pallas kernels: 91 us -> 92 us  [fused_shards(): pl.pallas_call(layer_kernel, out_shape=(jax.ShapeDtypeStruct((rows, cols)...]
where the time goes in v2:
time: 95.6 us; the launch traced here: 95.4 us
  Pallas kernels  92 us (96%)
  local copies, waits for them, and re-layouts  2.73 us (3%)
    pallas_call x1, Pallas kernels, fused_shards(): pl.pallas_call(layer_kernel, out_shape=(jax.ShapeDtypeStruct((rows, cols)...  92 us
    unnamed x2, local copies, waits for them, and re-layouts  2.73 us

profile of v2, /device:TPU:0, one launch (start us, length us, event | category | flops | bytes accessed | tf_op | source)
XLA Modules:
  0.0 95.4 jit_solution(8636015277353865076)
XLA Ops:
  0.6 92.0 %shard_map.122 = (bf16[128,640]{1,0:T(8,128)(2,1)}, f32[1,16]{1,0:T(1,128)}) custom-call(bf16[128,640]{1,0:T(8,128)(2,1)} %tokens.1, s32[6,128]{1,0:T(8,128)} %bitcast.8, f32[6,128]{1,0:T(8,128)} %bitcast.9, bf16[768,5120]{1,0:T(8,128)(2,1)} %bitcast.6, bf16[768,5120]{1,0:T(8,128)(2,1)} %bitcast.7, bf16[4,1536,640]{2,1,0:T(8,128)(2,1)} %w_down.1, ...), custom_call_target="tpu_custom_call" | custom-call | tf_op jit(solution)/shard_map/pallas_call | solution.py:479
  92.7 1.6 %copy.15 = bf16[128,640]{1,0:T(8,128)(2,1)} copy(bf16[128,640]{1,0:T(8,128)(2,1)} %get-tuple-element.8) | data formatting | bytes 327680
  94.3 1.1 %copy.16 = f32[16]{0:T(128)} copy(f32[16]{0:T(128)} %bitcast.11) | data formatting | bytes 128

commit v3 on v1

--- a/solution.py
+++ b/solution.py
@@ -323,6 +323,7 @@
     squeeze(far_rows, (0, 1))
     hs = silu_mul(sh_g[...], sh_u[...])
     hid[t, pl.ds(2 * far_rows, cap), :] = jnp.concatenate([hs[:cap], hs[cap:]], axis=1).astype(jnp.bfloat16)
+    hid_own.start()
     clear()
     chunks[3].relay_far()
     for c in (2, 3):
@@ -334,12 +335,13 @@
     for c in (2, 3):
         chunks[c].wait_y()
     up_seg(far_pair, chip_y, False)
+    hid_own.relay()
     for c in (2, 3):
         chunks[c].wait_far()
     up_seg(far_pair, chip_d, False)
     squeeze(0, (2, 3))
     hid_far.start()
-    hid_own.start()
+    hid_own.relay_far()
     for load in loads[5:]:
         load.wait()
 
@@ -393,13 +395,11 @@
     down_seg(0, chip_y, False)
     hid_far.wait_far()
     down_seg(0, chip_d, False)
-    hid_own.relay()
     give(2)
     give(3)
     out_acc[...] = jnp.zeros_like(out_acc)
     hid_own.wait_own()
     down_seg(far_rows, chip, True)
-    hid_own.relay_far()
     hid_own.wait_x()
     down_seg(far_rows, chip_x, True)
     hid_own.wait_y()

time: 94.6 us -> 92.1 us (0.974)
  Pallas kernels: 91 us -> 88.5 us
    pallas_call x1, Pallas kernels: 91 us -> 88.5 us  [fused_shards(): pl.pallas_call(layer_kernel, out_shape=(jax.ShapeDtypeStruct((rows, cols)...]
where the time goes in v3:
time: 92.1 us; the launch traced here: 91.9 us
  Pallas kernels  88.5 us (96%)
  local copies, waits for them, and re-layouts  2.73 us (3%)
    pallas_call x1, Pallas kernels, fused_shards(): pl.pallas_call(layer_kernel, out_shape=(jax.ShapeDtypeStruct((rows, cols)...  88.5 us
    unnamed x2, local copies, waits for them, and re-layouts  2.73 us

profile of v3, /device:TPU:0, one launch (start us, length us, event | category | flops | bytes accessed | tf_op | source)
XLA Modules:
  0.0 91.9 jit_solution(2424569402861623157)
XLA Ops:
  0.6 88.5 %shard_map.122 = (bf16[128,640]{1,0:T(8,128)(2,1)}, f32[1,16]{1,0:T(1,128)}) custom-call(bf16[128,640]{1,0:T(8,128)(2,1)} %tokens.1, s32[6,128]{1,0:T(8,128)} %bitcast.8, f32[6,128]{1,0:T(8,128)} %bitcast.9, bf16[768,5120]{1,0:T(8,128)(2,1)} %bitcast.6, bf16[768,5120]{1,0:T(8,128)(2,1)} %bitcast.7, bf16[4,1536,640]{2,1,0:T(8,128)(2,1)} %w_down.1, ...), custom_call_target="tpu_custom_call" | custom-call | tf_op jit(solution)/shard_map/pallas_call | solution.py:466
  89.2 1.6 %copy.15 = bf16[128,640]{1,0:T(8,128)(2,1)} copy(bf16[128,640]{1,0:T(8,128)(2,1)} %get-tuple-element.8) | data formatting | bytes 327680
  90.8 1.1 %copy.16 = f32[16]{0:T(128)} copy(f32[16]{0:T(128)} %bitcast.11) | data formatting | bytes 128
